TPU v7x, 32 devices: a whole 2x2x4 slice. The times are simulated.
32 devices in a mesh: req: 16 (over z, y, core), tp: 2 (over x).
Axes of the slice: x: 2, y: 2, z: 4, core: 2. Of those that a mesh axis runs over, the one named last changes fastest.
Arguments:
- text_stream: bfloat16 [16384, 4096], P('req', 'tp'), may hold values from -6 to 6
- image_rows: bfloat16 [8192, 4096], P('req', 'tp'), may hold values from -8 to 8
- positions: int32 [8192], P('req'), may hold values from 0 to 16383, as said below
- norm_gain: bfloat16 [4096], P('tp'), may hold values from 0.099609375 to 1.8984375
- kv_weight: bfloat16 [4096, 2048], P('tp'), may hold values from -0.125 to 0.125
Outputs:
- key_value: bfloat16 [2048, 16384], P('tp', 'req')
Inputs may be any that keep to these rules, and one draw needn't show every extreme that they name: All entries of positions are distinct. Among the image rows of one index of req, at most 64 have positions in the stream rows of any one index of req, and in every draw some index of req receives exactly that many from every index.
All inputs are finite; a program needn't handle non-finite values.
Results may differ from a plain program's by a relative error of at most 0.008.
Values may be sent and summed in bfloat16 or wider, within the bound.
A program may use at most 64 MiB of HBM per device.

v0:
```python
import functools

import jax
import jax.numpy as jnp
from jax import lax
from jax.experimental import pallas as pl
from jax.experimental.pallas import tpu as pltpu
from jax.sharding import PartitionSpec as P

EPSILON = 1e-05
LANES = 128
CHUNKS = 4
LATE = 1
EARLY = CHUNKS - LATE
MESH = pl.DeviceIdType.MESH
F32 = jnp.float32
BF16 = jnp.bfloat16


def iota(shape, dim):
    return lax.broadcasted_iota(jnp.int32, shape, dim)


def loop(start, stop, body):
    def step(i, carry):
        body(i)
        return carry

    lax.fori_loop(start, stop, step, 0)


def square_and_gain(x_ref, gain_ref, squares_ref):
    gain = gain_ref[...].astype(F32)

    def body(b):
        rows = pl.ds(pl.multiple_of(b * LANES, LANES), LANES)
        x = x_ref[rows, :].astype(F32)
        total = jnp.zeros((LANES, LANES), F32)
        for k in range(x.shape[1] // LANES):
            piece = x[:, k * LANES:(k + 1) * LANES]
            total = total + piece * piece
        squares_ref[b] = jnp.sum(total.T, axis=0, keepdims=True)
        x_ref[rows, :] = (x * gain).astype(BF16)

    loop(0, x_ref.shape[0] // LANES, body)


def kernel(
    n, width, pos_ref, gain_ref, img_hbm, text_hbm, w_hbm, out_hbm,
    img, text, w, pos_all, rank, p_send, p_recv, p_own, t_send, t_recv, t_own,
    u_send, u_recv, u_own,
    sq_img, sq_img_in, sq_text, sq_text_in, inv_img, pick, pack, arrived, place, outv,
    ld_sem, w_sem, pos_s, pos_r, sq_s, sq_r, p_s, p_r, t_s, t_r, u_s, u_r, a_s, a_r, o_sem,
):
    req, tp = lax.axis_index("req"), lax.axis_index("tp")
    peer = 1 - tp
    images, rows = img.shape[0], text.shape[0]
    cw = w.shape[3]
    half = CHUNKS * cw
    slots = place.shape[0]
    cap = slots // n

    def other(i):
        return lax.rem(req + i, n)

    def load_w(side, owner, c):
        return pltpu.make_async_copy(
            w_hbm.at[:, pl.ds(pl.multiple_of(owner * half + c * cw, cw), cw)], w.at[side, c], w_sem.at[side, c]
        )

    load_img = pltpu.make_async_copy(img_hbm, img, ld_sem.at[0])
    load_text = pltpu.make_async_copy(text_hbm, text, ld_sem.at[1])
    load_img.start()
    loop(0, CHUNKS, lambda c: load_w(0, peer, c).start())
    loop(EARLY, CHUNKS, lambda c: load_w(1, tp, c).start())
    load_text.start()
    loop(0, EARLY, lambda c: load_w(1, tp, c).start())

    barrier = pltpu.get_barrier_semaphore()
    loop(1, n, lambda i: pl.semaphore_signal(barrier, inc=1, device_id={"req": other(i)}, device_id_type=MESH))
    pl.semaphore_signal(barrier, inc=1, device_id={"tp": peer}, device_id_type=MESH)
    pl.semaphore_wait(barrier, n)

    def across(src, dst, send, recv):
        return pltpu.make_async_remote_copy(
            src_ref=src, dst_ref=dst, send_sem=send, recv_sem=recv, device_id={"tp": peer}, device_id_type=MESH
        )

    def pos_copy(i, source):
        return pltpu.make_async_remote_copy(
            src_ref=pos_all.at[source], dst_ref=pos_all.at[source], send_sem=pos_s.at[i],
            recv_sem=pos_r.at[source], device_id={"req": other(i)}, device_id_type=MESH,
        )

    pos_all[pl.ds(req, 1)] = pos_ref[...].reshape(1, 1, images)
    loop(1, n, lambda i: pos_copy(i, req).start())

    load_img.wait()
    square_and_gain(img, gain_ref, sq_img)
    copy_sq_img = across(sq_img, sq_img_in, sq_s.at[0], sq_r.at[0])
    copy_sq_img.start()

    def p_copy(c):
        return across(p_send.at[c], p_recv.at[c], p_s.at[c], p_r.at[c])

    def image_send(c):
        load_w(0, peer, c).wait()
        p_send[c] = jnp.dot(img[...], w[0, c], preferred_element_type=F32).astype(BF16)
        p_copy(c).start()

    loop(0, EARLY, image_send)

    row_pos = pos_ref[...]
    dest = iota((n, images), 0)
    member = (row_pos >= dest * rows) & (row_pos < (dest + 1) * rows)
    earlier = (iota((images, images), 0) < iota((images, images), 1)).astype(F32).astype(BF16)
    ones = member.astype(F32)
    before = jnp.dot(ones.astype(BF16), earlier, preferred_element_type=F32)
    target = jnp.sum((before + (dest * cap).astype(F32)) * ones, axis=0, keepdims=True)
    slot = iota((slots, images), 0).astype(F32)
    pick[...] = (slot == target).astype(F32).astype(BF16)

    copy_sq_img.wait()

    def inv_body(b):
        inv = lax.rsqrt((sq_img[b] + sq_img_in[b]) / width + EPSILON)
        inv_img[pl.ds(pl.multiple_of(b * LANES, LANES), LANES), :] = jnp.broadcast_to(inv, (LANES, LANES)).T

    loop(0, images // LANES, inv_body)

    def a_copy(c, i, dst, source):
        return pltpu.make_async_remote_copy(
            src_ref=pack.at[c, pl.ds(pl.multiple_of(dst * cap, cap), cap), :],
            dst_ref=arrived.at[c, pl.ds(pl.multiple_of(source * cap, cap), cap), :],
            send_sem=a_s.at[c, i], recv_sem=a_r.at[c, source],
            device_id={"req": other(i)}, device_id_type=MESH,
        )

    def pack_and_send(k, scaled):
        pack[k] = jnp.dot(pick[...], scaled, preferred_element_type=F32).astype(BF16)
        loop(1, n, lambda i: a_copy(k, i, other(i), req).start())
        mine = pl.ds(pl.multiple_of(req * cap, cap), cap)
        arrived[k, mine, :] = pack[k, mine, :]

    def scale(total):
        inv = inv_img[...]
        return jnp.concatenate(
            [total[:, k * LANES:(k + 1) * LANES] * inv for k in range(cw // LANES)], axis=1
        ).astype(BF16)

    def image_late(c):
        for side, owner, k in ((0, peer, CHUNKS - EARLY + c), (1, tp, c)):
            load_w(side, owner, c).wait()
            pack_and_send(k, scale(jnp.dot(img[...], w[side, c], preferred_element_type=F32)))

    loop(EARLY, CHUNKS, image_late)

    load_text.wait()
    square_and_gain(text, gain_ref, sq_text)

    def t_copy(c):
        return across(t_send.at[c], t_recv.at[c], t_s.at[c], t_r.at[c])

    def text_send(c):
        t_send[c] = jnp.dot(text[...], w[0, c], preferred_element_type=F32).astype(BF16)

    text_send(0)

    def image_own(c):
        load_w(1, tp, c).wait()
        p_own[c] = jnp.dot(img[...], w[1, c], preferred_element_type=F32)

    loop(0, EARLY, image_own)

    copy_sq_text = across(sq_text, sq_text_in, sq_s.at[1], sq_r.at[1])
    copy_sq_text.start()

    def image_pack(c):
        p_copy(c).wait_recv()
        t_copy(c).start()
        pack_and_send(c, scale(p_own[c] + p_recv[c].astype(F32)))

        @pl.when(c + 1 < EARLY)
        def _():
            text_send(c + 1)

    loop(0, EARLY, image_pack)

    loop(1, n, lambda i: pos_copy(i, other(i)).wait_recv())
    all_pos = pos_all[:, 0, :]
    local = all_pos - req * rows
    here = (local >= 0) & (local < rows)
    here_f = here.astype(F32)
    order = jnp.dot(here_f.astype(BF16), earlier, preferred_element_type=F32)
    rank[0] = jnp.where(here, order, -1.0)
    rank[1] = local.astype(F32) + 1.0

    def place_body(g):
        eight = pl.ds(pl.multiple_of(g * 8, 8), 8)
        order8 = rank[0, eight, :]
        local8 = rank[1, eight, :]
        for k in range(8):
            hit = iota((cap, images), 0).astype(F32) == order8[k:k + 1, :]
            at = jnp.sum(jnp.where(hit, local8[k:k + 1, :], 0.0), axis=1, keepdims=True)
            block = (iota((cap, rows), 1).astype(F32) + 1.0) == at
            place[pl.ds(pl.multiple_of((g * 8 + k) * cap, cap), cap), :] = block.astype(F32).astype(BF16)

    loop(0, n // 8, place_body)

    def text_own(c):
        t_own[c] = jnp.dot(text[...], w[1, c], preferred_element_type=F32)

    loop(0, CHUNKS, text_own)
    filled = jnp.max(place[...].astype(F32), axis=0, keepdims=True)

    def placed(k):
        loop(1, n, lambda i: a_copy(k, i, req, other(i)).wait_recv())
        return jnp.dot(arrived[k].T, place[...], preferred_element_type=F32)

    blocks = [slice(b * LANES, (b + 1) * LANES) for b in range(rows // LANES)]

    def u_copy(a):
        return across(u_send.at[a], u_recv.at[a], u_s.at[a], u_r.at[a])

    def merge_late(a):
        c = EARLY + a
        images_t = placed(CHUNKS + a)
        for at in blocks:
            part = jnp.dot(text[at, :], w[0, c], preferred_element_type=F32)
            u_send[a, :, at] = jnp.where(filled[:, at] > 0.5, images_t[:, at], part.T).astype(BF16)
        u_copy(a).start()
        images_t = placed(c)
        for at in blocks:
            u_own[a, :, at] = jnp.where(filled[:, at] > 0.5, images_t[:, at], t_own[c, at, :].T)

    loop(0, LATE, merge_late)
    copy_sq_text.wait()

    def out_copy(c):
        return pltpu.make_async_copy(
            outv.at[c], out_hbm.at[pl.ds(pl.multiple_of(c * cw, cw), cw), :], o_sem.at[c]
        )

    def text_inv(b):
        return lax.rsqrt((sq_text[b] + sq_text_in[b]) / width + EPSILON)

    def finish(c):
        images_t = placed(c)
        t_copy(c).wait_recv()
        for b, at in enumerate(blocks):
            texts = (t_own[c, at, :] + t_recv[c, at, :].astype(F32)).T * text_inv(b)
            outv[c, :, at] = jnp.where(filled[:, at] > 0.5, images_t[:, at], texts).astype(BF16)
        out_copy(c).start()

    loop(0, EARLY, finish)

    def finish_late(a):
        u_copy(a).wait_recv()
        for b, at in enumerate(blocks):
            inv = jnp.where(filled[:, at] > 0.5, 1.0, text_inv(b))
            outv[EARLY + a, :, at] = ((u_own[a, :, at] + u_recv[a, :, at].astype(F32)) * inv).astype(BF16)
        out_copy(EARLY + a).start()

    loop(0, LATE, finish_late)

    loop(1, n, lambda i: pos_copy(i, req).wait_send())
    loop(0, LATE, lambda a: u_copy(a).wait_send())
    loop(0, CHUNKS, lambda c: out_copy(c).wait())

    def drain(c):
        p_copy(c).wait_send()
        t_copy(c).wait_send()

    loop(0, EARLY, drain)
    loop(0, CHUNKS + LATE, lambda k: loop(1, n, lambda i: a_copy(k, i, other(i), req).wait_send()))


def local(text_stream, image_rows, positions, norm_gain, kv_weight):
    n, sides = lax.axis_size("req"), lax.axis_size("tp")
    rows, features = text_stream.shape
    images = image_rows.shape[0]
    half = kv_weight.shape[1] // sides
    cw = half // CHUNKS
    slots = 2 * images
    any_spec, vmem = pl.BlockSpec(memory_space=pl.ANY), pl.BlockSpec(memory_space=pltpu.VMEM)
    dma = pltpu.SemaphoreType.DMA
    return pl.pallas_call(
        functools.partial(kernel, n, features * sides),
        out_shape=jax.ShapeDtypeStruct((half, rows), BF16),
        in_specs=[vmem, vmem, any_spec, any_spec, any_spec],
        out_specs=any_spec,
        scratch_shapes=[
            pltpu.VMEM((images, features), BF16),
            pltpu.VMEM((rows, features), BF16),
            pltpu.VMEM((2, CHUNKS, features, cw), BF16),
            pltpu.VMEM((n, 1, images), jnp.int32),
            pltpu.VMEM((2, n, images), F32),
            pltpu.VMEM((EARLY, images, cw), BF16),
            pltpu.VMEM((EARLY, images, cw), BF16),
            pltpu.VMEM((EARLY, images, cw), F32),
            pltpu.VMEM((EARLY, rows, cw), BF16),
            pltpu.VMEM((EARLY, rows, cw), BF16),
            pltpu.VMEM((CHUNKS, rows, cw), F32),
            pltpu.VMEM((LATE, cw, rows), BF16),
            pltpu.VMEM((LATE, cw, rows), BF16),
            pltpu.VMEM((LATE, cw, rows), F32),
            pltpu.VMEM((images // LANES, 1, LANES), F32),
            pltpu.VMEM((images // LANES, 1, LANES), F32),
            pltpu.VMEM((rows // LANES, 1, LANES), F32),
            pltpu.VMEM((rows // LANES, 1, LANES), F32),
            pltpu.VMEM((images, LANES), F32),
            pltpu.VMEM((slots, images), BF16),
            pltpu.VMEM((CHUNKS + LATE, slots, cw), BF16),
            pltpu.VMEM((CHUNKS + LATE, slots, cw), BF16),
            pltpu.VMEM((slots, rows), BF16),
            pltpu.VMEM((CHUNKS, cw, rows), BF16),
            dma((2,)), dma((2, CHUNKS)), dma((n,)), dma((n,)), dma((2,)), dma((2,)),
            dma((EARLY,)), dma((EARLY,)), dma((EARLY,)), dma((EARLY,)), dma((LATE,)), dma((LATE,)),
            dma((CHUNKS + LATE, n)), dma((CHUNKS + LATE, n)), dma((CHUNKS,)),
        ],
        compiler_params=pltpu.CompilerParams(
            collective_id=0, has_side_effects=True, vmem_limit_bytes=56 * 1024 * 1024
        ),
        cost_estimate=pl.CostEstimate(
            flops=2 * (rows + images) * features * half * sides, bytes_accessed=16 << 20, transcendentals=0
        ),
    )(
        positions.reshape(1, images), norm_gain.reshape(1, features),
        image_rows, text_stream, kv_weight,
    )


def solution(mesh):
    return jax.shard_map(
        local,
        mesh=mesh,
        in_specs=(P("req", "tp"), P("req", "tp"), P("req"), P("tp"), P("tp", None)),
        out_specs=P("tp", "req"),
        check_vma=False,
    )
```

profile of v0, /device:TPU:0, one launch (start us, length us, event | category | flops | bytes accessed | tf_op | source)
XLA Modules:
  0.0 80.8 jit_solution(3481462640789177039)
XLA Ops:
  0.0 1.3 %reshape.7.gain_ref = bf16[1,2048]{1,0:T(2,128)(2,1)} reshape(bf16[2048]{0:T(1024)(128)(2,1)} %param.8) | data formatting | bytes 8192 | tf_op jit(solution)/shard_map/reshape | solution.py:328
  1.3 76.4 %shard_map.55 = bf16[1024,1024]{1,0:T(8,128)(2,1)} custom-call(s32[1,512]{1,0:T(1,128)} %bitcast.1, bf16[1,2048]{1,0:T(2,128)(2,1)} %reshape.7.gain_ref, bf16[512,2048]{1,0:T(8,128)(2,1)} %img_hbm.1, bf16[1024,2048]{1,0:T(8,128)(2,1)} %text_hbm.1, bf16[2048,2048]{1,0:T(8,128)(2,1)} %w_hbm.1), custom_call_target="tpu_custom_call" | custom-call | flops 12884901888 | bytes 16777216 | tf_op jit(solution)/shard_map/pallas_call | solution.py:287
  77.7 3.1 %copy.7 = bf16[1024,1024]{1,0:T(8,128)(2,1)} copy(bf16[1024,1024]{1,0:T(8,128)(2,1)} %shard_map.55) | data formatting | bytes 4194304
where the time goes:
time: 81 us; the launch traced here: 80.8 us
  Pallas kernels  76.4 us (94%)
  local copies, waits for them, and re-layouts  4.37 us (5%)
    pallas_call x1, Pallas kernels, local(): pl.pallas_call(functools.partial(kernel, n, features * sides), out_shape=...  76.4 us
    unnamed x1, local copies, waits for them, and re-layouts  3.08 us

commit v1 on v0

--- a/solution.py
+++ b/solution.py
@@ -29,29 +29,29 @@
     lax.fori_loop(start, stop, step, 0)
 
 
-def square_and_gain(x_ref, gain_ref, squares_ref):
-    gain = gain_ref[...].astype(F32)
-
+def squares(x_ref, squares_ref, gain_ref=None):
     def body(b):
         rows = pl.ds(pl.multiple_of(b * LANES, LANES), LANES)
-        x = x_ref[rows, :].astype(F32)
         total = jnp.zeros((LANES, LANES), F32)
-        for k in range(x.shape[1] // LANES):
-            piece = x[:, k * LANES:(k + 1) * LANES]
+        for k in range(x_ref.shape[1] // LANES):
+            piece = x_ref[rows, k * LANES:(k + 1) * LANES].astype(F32)
             total = total + piece * piece
         squares_ref[b] = jnp.sum(total.T, axis=0, keepdims=True)
-        x_ref[rows, :] = (x * gain).astype(BF16)
+        if gain_ref is not None:
+            x_ref[rows, :] = x_ref[rows, :] * gain_ref[...]
 
     loop(0, x_ref.shape[0] // LANES, body)
 
 
 def kernel(
     n, width, pos_ref, gain_ref, img_hbm, text_hbm, w_hbm, out_hbm,
-    img, text, w, pos_all, rank, p_send, p_recv, p_own, t_send, t_recv, t_own,
+    gain, raw, img, text, w, pos_all, rank, p_send, p_recv, p_own, t_send, t_recv, t_own,
     u_send, u_recv, u_own,
     sq_img, sq_img_in, sq_text, sq_text_in, inv_img, pick, pack, arrived, place, outv,
     ld_sem, w_sem, pos_s, pos_r, sq_s, sq_r, p_s, p_r, t_s, t_r, u_s, u_r, a_s, a_r, o_sem,
 ):
+    gain_row = gain_ref[...].reshape(1, gain_ref.shape[0])
+    gain[...] = gain_row
     req, tp = lax.axis_index("req"), lax.axis_index("tp")
     peer = 1 - tp
     images, rows = img.shape[0], text.shape[0]
@@ -68,13 +68,10 @@
             w_hbm.at[:, pl.ds(pl.multiple_of(owner * half + c * cw, cw), cw)], w.at[side, c], w_sem.at[side, c]
         )
 
-    load_img = pltpu.make_async_copy(img_hbm, img, ld_sem.at[0])
+    load_img = pltpu.make_async_copy(img_hbm, raw, ld_sem.at[0])
     load_text = pltpu.make_async_copy(text_hbm, text, ld_sem.at[1])
     load_img.start()
-    loop(0, CHUNKS, lambda c: load_w(0, peer, c).start())
-    loop(EARLY, CHUNKS, lambda c: load_w(1, tp, c).start())
-    load_text.start()
-    loop(0, EARLY, lambda c: load_w(1, tp, c).start())
+    load_w(0, peer, 0).start()
 
     barrier = pltpu.get_barrier_semaphore()
     loop(1, n, lambda i: pl.semaphore_signal(barrier, inc=1, device_id={"req": other(i)}, device_id_type=MESH))
@@ -96,9 +93,16 @@
     loop(1, n, lambda i: pos_copy(i, req).start())
 
     load_img.wait()
-    square_and_gain(img, gain_ref, sq_img)
-    copy_sq_img = across(sq_img, sq_img_in, sq_s.at[0], sq_r.at[0])
-    copy_sq_img.start()
+    loop(1, CHUNKS, lambda c: load_w(0, peer, c).start())
+    load_text.start()
+    loop(EARLY, CHUNKS, lambda c: load_w(1, tp, c).start())
+    loop(0, EARLY, lambda c: load_w(1, tp, c).start())
+
+    def gain_body(b):
+        at = pl.ds(pl.multiple_of(b * LANES, LANES), LANES)
+        img[at, :] = raw[at, :] * gain[...]
+
+    loop(0, images // LANES, gain_body)
 
     def p_copy(c):
         return across(p_send.at[c], p_recv.at[c], p_s.at[c], p_r.at[c])
@@ -108,7 +112,11 @@
         p_send[c] = jnp.dot(img[...], w[0, c], preferred_element_type=F32).astype(BF16)
         p_copy(c).start()
 
-    loop(0, EARLY, image_send)
+    image_send(0)
+    squares(raw, sq_img)
+    copy_sq_img = across(sq_img, sq_img_in, sq_s.at[0], sq_r.at[0])
+    copy_sq_img.start()
+    loop(1, EARLY, image_send)
 
     row_pos = pos_ref[...]
     dest = iota((n, images), 0)
@@ -148,15 +156,14 @@
             [total[:, k * LANES:(k + 1) * LANES] * inv for k in range(cw // LANES)], axis=1
         ).astype(BF16)
 
-    def image_late(c):
-        for side, owner, k in ((0, peer, CHUNKS - EARLY + c), (1, tp, c)):
-            load_w(side, owner, c).wait()
-            pack_and_send(k, scale(jnp.dot(img[...], w[side, c], preferred_element_type=F32)))
-
-    loop(EARLY, CHUNKS, image_late)
+    def image_late(side, owner, c, k):
+        load_w(side, owner, c).wait()
+        pack_and_send(k, scale(jnp.dot(img[...], w[side, c], preferred_element_type=F32)))
+
+    loop(0, LATE, lambda a: image_late(0, peer, EARLY + a, CHUNKS + a))
 
     load_text.wait()
-    square_and_gain(text, gain_ref, sq_text)
+    squares(text, sq_text, gain)
 
     def t_copy(c):
         return across(t_send.at[c], t_recv.at[c], t_s.at[c], t_r.at[c])
@@ -165,6 +172,7 @@
         t_send[c] = jnp.dot(text[...], w[0, c], preferred_element_type=F32).astype(BF16)
 
     text_send(0)
+    loop(EARLY, CHUNKS, lambda c: image_late(1, tp, c, c))
 
     def image_own(c):
         load_w(1, tp, c).wait()
@@ -207,10 +215,6 @@
 
     loop(0, n // 8, place_body)
 
-    def text_own(c):
-        t_own[c] = jnp.dot(text[...], w[1, c], preferred_element_type=F32)
-
-    loop(0, CHUNKS, text_own)
     filled = jnp.max(place[...].astype(F32), axis=0, keepdims=True)
 
     def placed(k):
@@ -229,11 +233,20 @@
             part = jnp.dot(text[at, :], w[0, c], preferred_element_type=F32)
             u_send[a, :, at] = jnp.where(filled[:, at] > 0.5, images_t[:, at], part.T).astype(BF16)
         u_copy(a).start()
+
+    loop(0, LATE, merge_late)
+
+    def text_own(c):
+        t_own[c] = jnp.dot(text[...], w[1, c], preferred_element_type=F32)
+
+    loop(0, CHUNKS, text_own)
+
+    def own_late(a):
+        c = EARLY + a
         images_t = placed(c)
         for at in blocks:
             u_own[a, :, at] = jnp.where(filled[:, at] > 0.5, images_t[:, at], t_own[c, at, :].T)
 
-    loop(0, LATE, merge_late)
     copy_sq_text.wait()
 
     def out_copy(c):
@@ -244,15 +257,20 @@
     def text_inv(b):
         return lax.rsqrt((sq_text[b] + sq_text_in[b]) / width + EPSILON)
 
-    def finish(c):
-        images_t = placed(c)
+    def finish_text(c):
         t_copy(c).wait_recv()
         for b, at in enumerate(blocks):
             texts = (t_own[c, at, :] + t_recv[c, at, :].astype(F32)).T * text_inv(b)
-            outv[c, :, at] = jnp.where(filled[:, at] > 0.5, images_t[:, at], texts).astype(BF16)
+            outv[c, :, at] = texts.astype(BF16)
+
+    def finish_images(c):
+        images_t = placed(c)
+        outv[c] = jnp.where(filled > 0.5, images_t, outv[c].astype(F32)).astype(BF16)
         out_copy(c).start()
 
-    loop(0, EARLY, finish)
+    loop(0, EARLY, finish_text)
+    loop(0, LATE, own_late)
+    loop(0, EARLY, finish_images)
 
     def finish_late(a):
         u_copy(a).wait_recv()
@@ -290,6 +308,8 @@
         in_specs=[vmem, vmem, any_spec, any_spec, any_spec],
         out_specs=any_spec,
         scratch_shapes=[
+            pltpu.VMEM((1, features), BF16),
+            pltpu.VMEM((images, features), BF16),
             pltpu.VMEM((images, features), BF16),
             pltpu.VMEM((rows, features), BF16),
             pltpu.VMEM((2, CHUNKS, features, cw), BF16),
@@ -325,7 +345,7 @@
             flops=2 * (rows + images) * features * half * sides, bytes_accessed=16 << 20, transcendentals=0
         ),
     )(
-        positions.reshape(1, images), norm_gain.reshape(1, features),
+        positions.reshape(1, images), norm_gain,
         image_rows, text_stream, kv_weight,
     )
 

time: 81 us -> 80.8 us (level); the launches traced: 80.8 us -> 79.2 us
  local copies, waits for them, and re-layouts: 4.37 us -> 3.08 us
    reshape x1 -> x0, local copies, waits for them, and re-layouts: 1.29 us -> none  [local(): norm_gain.reshape(1, features)]
where the time goes in v1:
time: 80.8 us; the launch traced here: 79.2 us
  Pallas kernels  76.1 us (94%)
  local copies, waits for them, and re-layouts  3.08 us (4%)
    pallas_call x1, Pallas kernels, local(): pl.pallas_call(functools.partial(kernel, n, features * sides), out_shape=...  76.1 us
    unnamed x1, local copies, waits for them, and re-layouts  3.08 us

profile of v1, /device:TPU:0, one launch (start us, length us, event | category | flops | bytes accessed | tf_op | source)
XLA Modules:
  0.0 79.2 jit_solution(14170912917690849858)
XLA Ops:
  0.0 76.1 %shard_map.55 = bf16[1024,1024]{1,0:T(8,128)(2,1)} custom-call(s32[1,512]{1,0:T(1,128)} %bitcast.1, bf16[2048]{0:T(1024)(128)(2,1)} %gain_ref.1, bf16[512,2048]{1,0:T(8,128)(2,1)} %img_hbm.1, bf16[1024,2048]{1,0:T(8,128)(2,1)} %text_hbm.1, bf16[2048,2048]{1,0:T(8,128)(2,1)} %w_hbm.1), custom_call_target="tpu_custom_call" | custom-call | flops 12884901888 | bytes 16777216 | tf_op jit(solution)/shard_map/pallas_call | solution.py:305
  76.1 3.1 %copy.7 = bf16[1024,1024]{1,0:T(8,128)(2,1)} copy(bf16[1024,1024]{1,0:T(8,128)(2,1)} %shard_map.55) | data formatting | bytes 4194304

commit v2 on v1

--- a/solution.py
+++ b/solution.py
@@ -29,7 +29,7 @@
     lax.fori_loop(start, stop, step, 0)
 
 
-def squares(x_ref, squares_ref, gain_ref=None):
+def squares(x_ref, squares_ref):
     def body(b):
         rows = pl.ds(pl.multiple_of(b * LANES, LANES), LANES)
         total = jnp.zeros((LANES, LANES), F32)
@@ -37,15 +37,21 @@
             piece = x_ref[rows, k * LANES:(k + 1) * LANES].astype(F32)
             total = total + piece * piece
         squares_ref[b] = jnp.sum(total.T, axis=0, keepdims=True)
-        if gain_ref is not None:
-            x_ref[rows, :] = x_ref[rows, :] * gain_ref[...]
+
+    loop(0, x_ref.shape[0] // LANES, body)
+
+
+def gained(x_ref, gain_ref, out_ref):
+    def body(b):
+        at = pl.ds(pl.multiple_of(b * LANES, LANES), LANES)
+        out_ref[at, :] = x_ref[at, :] * gain_ref[...]
 
     loop(0, x_ref.shape[0] // LANES, body)
 
 
 def kernel(
     n, width, pos_ref, gain_ref, img_hbm, text_hbm, w_hbm, out_hbm,
-    gain, raw, img, text, w, pos_all, rank, p_send, p_recv, p_own, t_send, t_recv, t_own,
+    gain, raw, img, raw_text, text, w, pos_all, rank, p_send, p_recv, p_own, t_send, t_recv, t_own,
     u_send, u_recv, u_own,
     sq_img, sq_img_in, sq_text, sq_text_in, inv_img, pick, pack, arrived, place, outv,
     ld_sem, w_sem, pos_s, pos_r, sq_s, sq_r, p_s, p_r, t_s, t_r, u_s, u_r, a_s, a_r, o_sem,
@@ -69,7 +75,7 @@
         )
 
     load_img = pltpu.make_async_copy(img_hbm, raw, ld_sem.at[0])
-    load_text = pltpu.make_async_copy(text_hbm, text, ld_sem.at[1])
+    load_text = pltpu.make_async_copy(text_hbm, raw_text, ld_sem.at[1])
     load_img.start()
     load_w(0, peer, 0).start()
 
@@ -98,11 +104,7 @@
     loop(EARLY, CHUNKS, lambda c: load_w(1, tp, c).start())
     loop(0, EARLY, lambda c: load_w(1, tp, c).start())
 
-    def gain_body(b):
-        at = pl.ds(pl.multiple_of(b * LANES, LANES), LANES)
-        img[at, :] = raw[at, :] * gain[...]
-
-    loop(0, images // LANES, gain_body)
+    gained(raw, gain, img)
 
     def p_copy(c):
         return across(p_send.at[c], p_recv.at[c], p_s.at[c], p_r.at[c])
@@ -161,31 +163,27 @@
         pack_and_send(k, scale(jnp.dot(img[...], w[side, c], preferred_element_type=F32)))
 
     loop(0, LATE, lambda a: image_late(0, peer, EARLY + a, CHUNKS + a))
+    loop(EARLY, CHUNKS, lambda c: image_late(1, tp, c, c))
 
     load_text.wait()
-    squares(text, sq_text, gain)
+    gained(raw_text, gain, text)
 
     def t_copy(c):
         return across(t_send.at[c], t_recv.at[c], t_s.at[c], t_r.at[c])
 
     def text_send(c):
         t_send[c] = jnp.dot(text[...], w[0, c], preferred_element_type=F32).astype(BF16)
+        t_copy(c).start()
 
     text_send(0)
-    loop(EARLY, CHUNKS, lambda c: image_late(1, tp, c, c))
-
     def image_own(c):
         load_w(1, tp, c).wait()
         p_own[c] = jnp.dot(img[...], w[1, c], preferred_element_type=F32)
 
     loop(0, EARLY, image_own)
 
-    copy_sq_text = across(sq_text, sq_text_in, sq_s.at[1], sq_r.at[1])
-    copy_sq_text.start()
-
     def image_pack(c):
         p_copy(c).wait_recv()
-        t_copy(c).start()
         pack_and_send(c, scale(p_own[c] + p_recv[c].astype(F32)))
 
         @pl.when(c + 1 < EARLY)
@@ -228,13 +226,16 @@
 
     def merge_late(a):
         c = EARLY + a
+        t_own[c] = jnp.dot(text[...], w[0, c], preferred_element_type=F32)
         images_t = placed(CHUNKS + a)
         for at in blocks:
-            part = jnp.dot(text[at, :], w[0, c], preferred_element_type=F32)
-            u_send[a, :, at] = jnp.where(filled[:, at] > 0.5, images_t[:, at], part.T).astype(BF16)
+            u_send[a, :, at] = jnp.where(filled[:, at] > 0.5, images_t[:, at], t_own[c, at, :].T).astype(BF16)
         u_copy(a).start()
 
     loop(0, LATE, merge_late)
+    squares(raw_text, sq_text)
+    copy_sq_text = across(sq_text, sq_text_in, sq_s.at[1], sq_r.at[1])
+    copy_sq_text.start()
 
     def text_own(c):
         t_own[c] = jnp.dot(text[...], w[1, c], preferred_element_type=F32)
@@ -311,6 +312,7 @@
             pltpu.VMEM((1, features), BF16),
             pltpu.VMEM((images, features), BF16),
             pltpu.VMEM((images, features), BF16),
+            pltpu.VMEM((rows, features), BF16),
             pltpu.VMEM((rows, features), BF16),
             pltpu.VMEM((2, CHUNKS, features, cw), BF16),
             pltpu.VMEM((n, 1, images), jnp.int32),

time: 80.8 us -> 83.6 us (1.035); the launches traced: 79.2 us -> 83.4 us
  Pallas kernels: 76.1 us -> 80.3 us
    pallas_call x1, Pallas kernels: 76.1 us -> 80.3 us  [local(): pl.pallas_call(functools.partial(kernel, n, features * sides), out_shape=...]
where the time goes in v2:
time: 83.6 us; the launch traced here: 83.4 us
  Pallas kernels  80.3 us (96%)
  local copies, waits for them, and re-layouts  3.08 us (4%)
    pallas_call x1, Pallas kernels, local(): pl.pallas_call(functools.partial(kernel, n, features * sides), out_shape=...  80.3 us
    unnamed x1, local copies, waits for them, and re-layouts  3.08 us

profile of v2, /device:TPU:0, one launch (start us, length us, event | category | flops | bytes accessed | tf_op | source)
XLA Modules:
  0.0 83.4 jit_solution(375050546112398599)
XLA Ops:
  0.0 80.3 %shard_map.55 = bf16[1024,1024]{1,0:T(8,128)(2,1)} custom-call(s32[1,512]{1,0:T(1,128)} %bitcast.1, bf16[2048]{0:T(1024)(128)(2,1)} %gain_ref.1, bf16[512,2048]{1,0:T(8,128)(2,1)} %img_hbm.1, bf16[1024,2048]{1,0:T(8,128)(2,1)} %text_hbm.1, bf16[2048,2048]{1,0:T(8,128)(2,1)} %w_hbm.1), custom_call_target="tpu_custom_call" | custom-call | flops 12884901888 | bytes 16777216 | tf_op jit(solution)/shard_map/pallas_call | solution.py:306
  80.3 3.1 %copy.7 = bf16[1024,1024]{1,0:T(8,128)(2,1)} copy(bf16[1024,1024]{1,0:T(8,128)(2,1)} %shard_map.55) | data formatting | bytes 4194304

commit v3 on v2

--- a/solution.py
+++ b/solution.py
@@ -173,24 +173,28 @@
 
     def text_send(c):
         t_send[c] = jnp.dot(text[...], w[0, c], preferred_element_type=F32).astype(BF16)
-        t_copy(c).start()
-
-    text_send(0)
     def image_own(c):
         load_w(1, tp, c).wait()
         p_own[c] = jnp.dot(img[...], w[1, c], preferred_element_type=F32)
 
     loop(0, EARLY, image_own)
+    text_send(0)
 
     def image_pack(c):
         p_copy(c).wait_recv()
+
+        @pl.when(c == EARLY - 1)
+        def _():
+            t_copy(0).start()
+
         pack_and_send(c, scale(p_own[c] + p_recv[c].astype(F32)))
 
-        @pl.when(c + 1 < EARLY)
-        def _():
-            text_send(c + 1)
+    def text_rest(c):
+        text_send(c)
+        t_copy(c).start()
 
     loop(0, EARLY, image_pack)
+    loop(1, EARLY, text_rest)
 
     loop(1, n, lambda i: pos_copy(i, other(i)).wait_recv())
     all_pos = pos_all[:, 0, :]

time: 83.6 us -> 84.6 us (1.012)
  Pallas kernels: 80.3 us -> 81.3 us
    pallas_call x1, Pallas kernels: 80.3 us -> 81.3 us  [local(): pl.pallas_call(functools.partial(kernel, n, features * sides), out_shape=...]
where the time goes in v3:
time: 84.6 us; the launch traced here: 84.4 us
  Pallas kernels  81.3 us (96%)
  local copies, waits for them, and re-layouts  3.08 us (4%)
    pallas_call x1, Pallas kernels, local(): pl.pallas_call(functools.partial(kernel, n, features * sides), out_shape=...  81.3 us
    unnamed x1, local copies, waits for them, and re-layouts  3.08 us

profile of v3, /device:TPU:0, one launch (start us, length us, event | category | flops | bytes accessed | tf_op | source)
XLA Modules:
  0.0 84.4 jit_solution(17715788759077859276)
XLA Ops:
  0.0 81.3 %shard_map.55 = bf16[1024,1024]{1,0:T(8,128)(2,1)} custom-call(s32[1,512]{1,0:T(1,128)} %bitcast.1, bf16[2048]{0:T(1024)(128)(2,1)} %gain_ref.1, bf16[512,2048]{1,0:T(8,128)(2,1)} %img_hbm.1, bf16[1024,2048]{1,0:T(8,128)(2,1)} %text_hbm.1, bf16[2048,2048]{1,0:T(8,128)(2,1)} %w_hbm.1), custom_call_target="tpu_custom_call" | custom-call | flops 12884901888 | bytes 16777216 | tf_op jit(solution)/shard_map/pallas_call | solution.py:310
  81.4 3.1 %copy.7 = bf16[1024,1024]{1,0:T(8,128)(2,1)} copy(bf16[1024,1024]{1,0:T(8,128)(2,1)} %shard_map.55) | data formatting | bytes 4194304
